TPU v7x, 32 devices: a whole 2x2x4 slice. The times are simulated.
32 devices in a mesh: win: 2 (over y), sta: 4 (over z), seg: 2 (over x), frq: 2 (over core).
Axes of the slice: x: 2, y: 2, z: 4, core: 2. Of those that a mesh axis runs over, the one named last changes fastest.
Arguments:
- ingest: bfloat16 [4, 2048, 512], P(('win', 'seg'), 'sta'), parts along dimension 0
- seg_offsets: int32 [4], P(('win', 'seg')), parts along dimension 0, may hold values from 0 to 2047
- pair_blocks: int32 [2, 24], P(None, 'sta'), may hold values from 0 to 63, as said below
- pair_count: int32 [4], P('sta'), may hold values from 1 to 6, as said below
Outputs:
- correlations: float32 [1200, 3072], P(('seg', 'frq'), ('win', 'sta')), parts along dimension 1
There are 2 independent parts, one for each index of `win`. A program takes and returns all parts, laid end to end along the dimension named above; an argument that names none is the same for every part. Nothing has to cross between parts.
Inputs may be any that keep to these rules, and one draw needn't show every extreme that they name: `pair_count`: each owner's number of live slots; they sum to exactly 12, and some owner has exactly 6. `pair_blocks`: column q lists the blocks of slot q, owned by q // 6; row 0 names a block that this owner holds, (q // 6) * 16 to that plus 16 - 1; row 1 names any block; of one owner's 6 slots at most 2 have their second block on any one owner, and some owner holds exactly 2 of them; the second blocks of the owners' first slots lie on distinct owners.
All inputs are finite; a program needn't handle non-finite values.
Results may differ from a plain program's by a relative error of at most 0.0054.
Values may be sent and summed in bfloat16 or wider, within the bound.
A program may use at most 64 MiB of HBM per device.

v0:
```python
import math

import jax
import jax.numpy as jnp
from jax import lax
from jax.sharding import PartitionSpec as P

MAXLAG = 600
BLOCK_STA = 8
HOLD_CAP = 2


HALF_TAPS = 10
NOISE_BASELINE = 0.5


def whiten(traces):
    spectral_magnitude = jnp.abs(traces.astype(jnp.float32))
    padded = jnp.pad(spectral_magnitude, ((0, 0), (HALF_TAPS, HALF_TAPS), (0, 0)))
    record_span_duration = traces.shape[1]
    levels = padded[:, 0:record_span_duration, :]
    for shift_step in range(1, 2 * HALF_TAPS + 1):
        levels = levels + padded[:, shift_step : shift_step + record_span_duration, :]
    levels = levels / (2 * HALF_TAPS + 1)
    return (traces.astype(jnp.float32) / jnp.maximum(levels, NOISE_BASELINE)).astype(jnp.bfloat16)


def dft_table(first_bin, bin_count, record_span_duration):
    oscillation_duration = 2 * record_span_duration
    fourier_mode_number = first_bin + jnp.arange(bin_count, dtype=jnp.int32)
    recording_moments = jnp.arange(record_span_duration, dtype=jnp.int32)
    rotation_increment_number = (
        fourier_mode_number[:, None] * recording_moments[None, :] % oscillation_duration
    )
    angles = rotation_increment_number.astype(jnp.float32) * (2.0 * math.pi / oscillation_duration)
    return jnp.concatenate([jnp.cos(angles), -jnp.sin(angles)], 0).astype(jnp.bfloat16)


def lag_offsets_table(lag_count, first_bin, bin_count, record_span_duration, segments, max_lag):
    oscillation_duration = 2 * record_span_duration
    lag_values = jnp.arange(lag_count, dtype=jnp.int32) - max_lag
    fourier_mode_number = first_bin + jnp.arange(bin_count, dtype=jnp.int32)
    rotation_increment_number = (
        fourier_mode_number[None, :]
        * (lag_values[:, None] % oscillation_duration)
        % oscillation_duration
    )
    angles = rotation_increment_number.astype(jnp.float32) * (2.0 * math.pi / oscillation_duration)
    weights = jnp.where(fourier_mode_number == 0, 1.0, 2.0).astype(jnp.float32)[None, :]
    norm_scale = 1.0 / (oscillation_duration * math.sqrt(record_span_duration * segments))
    return jnp.concatenate([jnp.cos(angles) * weights, -jnp.sin(angles) * weights], 1) * norm_scale


def cross_spectra(first_spectra, second_spectra, live_mask):
    real_part = jnp.einsum(
        "gkpi,gkpj->kpij",
        first_spectra[:, 0],
        second_spectra[:, 0],
        preferred_element_type=jnp.float32,
    ) + jnp.einsum(
        "gkpi,gkpj->kpij",
        first_spectra[:, 1],
        second_spectra[:, 1],
        preferred_element_type=jnp.float32,
    )
    imag_part = jnp.einsum(
        "gkpi,gkpj->kpij",
        first_spectra[:, 1],
        second_spectra[:, 0],
        preferred_element_type=jnp.float32,
    ) - jnp.einsum(
        "gkpi,gkpj->kpij",
        first_spectra[:, 0],
        second_spectra[:, 1],
        preferred_element_type=jnp.float32,
    )
    stacked = jnp.concatenate([real_part, imag_part], 0) * live_mask[None, :, None, None]
    return stacked.reshape(stacked.shape[0], -1)


def lag_sums(cross_terms, first_bin, record_span_duration, segments):
    groups = lax.axis_size(("seg", "frq"))
    per_device = 2 * MAXLAG // groups
    bin_count = cross_terms.shape[0] // 2
    lag_rows = lag_offsets_table(
        lax.axis_size(("seg", "frq")) * per_device,
        first_bin,
        bin_count,
        record_span_duration,
        segments,
        MAXLAG,
    )
    return lax.psum_scatter(
        jnp.dot(
            lag_rows,
            cross_terms,
            precision=lax.Precision.HIGHEST,
            preferred_element_type=jnp.float32,
        ),
        ("seg", "frq"),
        scatter_dimension=0,
        tiled=True,
    )


def on_device(ingest, seg_offsets, pair_blocks, pair_count):
    arrived = lax.all_to_all(ingest, "sta", split_axis=2, concat_axis=1, tiled=True)
    seg_local, record_span_duration, sta_local = arrived.shape
    traces = jax.vmap(lambda buffer_rows, offset: jnp.roll(buffer_rows, -offset, axis=0))(
        arrived, seg_offsets
    )
    whitened = whiten(traces)
    band_count = record_span_duration // lax.axis_size("frq")
    first_bin = lax.axis_index("frq") * band_count
    twiddles = dft_table(first_bin, band_count, record_span_duration)
    spectra = jnp.einsum(
        "kt,gts->gks", twiddles, whitened, preferred_element_type=jnp.float32
    ).astype(jnp.bfloat16)
    spectra = spectra.reshape(seg_local, 2, band_count, sta_local)
    block_width = BLOCK_STA
    own_blocks = sta_local // block_width
    own_view = spectra.reshape(seg_local, 2, band_count, own_blocks, block_width)
    owners = lax.axis_size("sta")
    owner_index = lax.axis_index("sta")
    segments = seg_local * lax.axis_size("seg")
    slot_count = pair_blocks.shape[1]
    live_mask = (jnp.arange(slot_count, dtype=jnp.int32) < pair_count[0]).astype(jnp.float32)
    first_spectra = jnp.take(own_view, pair_blocks[0] - owner_index * own_blocks, axis=3)
    block_ids = pair_blocks[1]
    capacity = min(HOLD_CAP, slot_count)
    wanted = block_ids.shape[0]
    holder = block_ids // own_blocks
    inside = block_ids % own_blocks
    positions = jnp.arange(wanted, dtype=jnp.int32)
    same_holder = holder[:, None] == holder[None, :]
    earlier = positions[None, :] < positions[:, None]
    rank = jnp.sum((same_holder & earlier).astype(jnp.int32), axis=1)
    owner_ids = jnp.arange(owners, dtype=jnp.int32)
    rank_ids = jnp.arange(capacity, dtype=jnp.int32)
    matches = (holder[None, None, :] == owner_ids[:, None, None]) & (
        rank[None, None, :] == rank_ids[None, :, None]
    )
    requests = jnp.sum(jnp.where(matches, inside[None, None, :], 0), axis=2)
    asked_rows = lax.all_to_all(requests, "sta", split_axis=0, concat_axis=0, tiled=True)
    replies = jnp.take(own_view, asked_rows.reshape(-1), axis=3)
    replies = replies.reshape(seg_local, 2, band_count, owners * capacity * block_width)
    returned = lax.all_to_all(replies, "sta", split_axis=3, concat_axis=3, tiled=True)
    returned = returned.reshape(seg_local, 2, band_count, owners * capacity, block_width)
    second_spectra = jnp.take(returned, holder * capacity + rank, axis=3)
    cross_terms = cross_spectra(first_spectra, second_spectra, live_mask)
    return lag_sums(cross_terms, first_bin, record_span_duration, segments)


def solution(mesh):
    placed = (P(("win", "seg"), "sta", None), P(("win", "seg")), P(None, "sta"), P("sta"))
    return jax.shard_map(
        on_device,
        mesh=mesh,
        in_specs=placed,
        out_specs=P(("seg", "frq"), ("win", "sta")),
        check_vma=False,
    )
```

profile of v0, /device:TPU:0, one launch (start us, length us, event | category | flops | bytes accessed | tf_op | source)
XLA Modules:
  0.0 162.2 jit_solution(8349814003379252261)
XLA Ops:
  0.0 0.7 and_select_fusion.3
  0.7 0.7 fusion.49
  1.4 0.2 convert_reduce_fusion
  1.6 0.1 select_reduce_fusion
  1.7 0.7 copy.28
  2.4 6.3 %all-to-all-start.1 = ((s32[4,1,2]{2,1,0:T(1,128)}), s32[4,1,2]{2,1,0:T(1,128)S(1)}, u32[]{:S(2)}, u32[]{:S(2)}) async-start(s32[4,1,2]{2,1,0:T(1,128)} %copy.28), calls=%async_computation.1 | async-start | bytes 4096 | tf_op jit(solution)/shard_map/all_to_all | solution.py:144
  8.8 2.4 %copy.26 = bf16[1,512,512]{1,0,2:T(2,128)(2,1)S(1)} copy(bf16[1,512,512]{2,1,0:T(8,128)(2,1)} %param.4) | data formatting | bytes 1048576 | tf_op args[0]
  11.2 0.5 broadcast.494
  11.7 3.7 %reduce.6 = bf16[512,512]{1,0:T(8,128)(2,1)S(1)} reduce(bf16[512,1,512]{2,1,0:T(2,128)(2,1)S(1)} %bitcast.102, bf16[]{:T(256)} %broadcast.494), dimensions={1}, to_apply=%bitcast.91.reduce_sub_computation | reduce | bytes 1048578
  15.4 0.0 copy-start
  15.5 1.2 reshape.483
  16.6 36.8 %cosine_convert_fusion = (bf16[1024,2048]{1,0:T(8,128)(2,1)}, bf16[1024,2048]{1,0:T(8,128)(2,1)}) fusion(s32[1024]{0:T(1024)S(1)} %iota_add_fusion), kind=kLoop, calls=%fused_computation.21 | loop fusion | flops 35651584 | bytes 8392704 | tf_op jit(solution)/shard_map/convert.16
  53.5 22.0 %cosine_multiply_fusion = (f32[1200,1024]{1,0:T(8,128)}, f32[1200,1024]{1,0:T(8,128)}) fusion(f32[1024]{0:T(1024)S(1)} %compare_select_fusion, s32[1200]{0:T(1024)S(1)} %add_select_fusion.2, s32[1024]{0:T(1024)S(1)} %iota_add_fusion), kind=kLoop, calls=%fused_computation.32 | loop fusion | flops 20889600 | bytes 9843392 | tf_op jit(solution)/shard_map/mul | solution.py:51
  75.5 0.0 all-to-all-done.1
  75.5 5.1 %all-to-all-start = ((bf16[4,2,32768]{2,1,0:T(2,128)(2,1)}), bf16[4,2,32768]{2,1,0:T(2,128)(2,1)S(1)}, u32[]{:S(2)}, u32[]{:S(2)}) async-start(bf16[4,2,32768]{2,1,0:T(2,128)(2,1)} %reshape.483), calls=%async_computation | async-start | bytes 1048576 | tf_op jit(solution)/shard_map/all_to_all | solution.py:107
  81.9 0.1 reshape.402
  82.0 0.5 broadcast.493
  82.5 0.7 reduce.5
  83.2 0.1 reshape.401
  83.3 0.1 broadcast_in_dim.79
  83.4 0.1 broadcast_in_dim.80
  83.5 11.0 %all-to-all-done = bf16[4,2,32768]{2,1,0:T(2,128)(2,1)S(1)} async-done(((bf16[4,2,32768]{2,1,0:T(2,128)(2,1)}), bf16[4,2,32768]{2,1,0:T(2,128)(2,1)S(1)}, u32[]{:S(2)}, u32[]{:S(2)}) %all-to-all-start) | async-done | bytes 524320 | tf_op jit(solution)/shard_map/all_to_all | solution.py:107
  94.5 0.5 reshape.484
  95.0 0.1 copy.33
  95.2 0.3 copy.27
  95.4 2.0 %convert_abs_fusion = f32[1,2048,128]{2,1,0:T(8,128)S(1)} fusion(s32[]{:T(128)} %bitcast.3, bf16[1,2048,128]{2,1,0:T(8,128)(2,1)S(1)} %bitcast.104), kind=kLoop, calls=%fused_computation.41 | loop fusion | flops 1310720 | bytes 1572868 | tf_op jit(solution)/shard_map/abs | solution.py:18
  97.4 7.5 %fusion.20 = bf16[128,2048]{1,0:T(8,128)(2,1)S(1)} fusion(bf16[1024,2048]{1,0:T(8,128)(2,1)} %get-tuple-element.27, bf16[1024,2048]{1,0:T(8,128)(2,1)} %get-tuple-element.26, f32[1,2048,128]{2,1,0:T(8,128)S(1)} %convert_abs_fusion, s32[]{:T(128)} %bitcast.3, bf16[1,2048,128]{2,1,0:T(8,128)(2,1)S(1)} %bitcast.105), kind=kOutput, calls=%fused_computation.36 | convolution fusion | flops 1098121216 | bytes 10485764 | tf_op jit(solution)/shard_map/kt,gts->gks/dot_general | solution.py:116
  104.9 0.6 gather_fusion.1
  105.5 0.1 bitcast_select_fusion
  105.6 1.0 copy.31
  106.6 3.6 %all-to-all-start.2 = ((bf16[1,2,1024,64]{2,1,0,3:T(2,128)(2,1)}), bf16[1,2,1024,64]{2,1,0,3:T(2,128)(2,1)S(1)}, u32[]{:S(2)}, u32[]{:S(2)}) async-start(bf16[1,2,1024,64]{2,1,0,3:T(2,128)(2,1)} %copy.31), calls=%async_computation.2 | async-start | bytes 524288 | tf_op jit(solution)/shard_map/all_to_all | solution.py:147
  110.2 0.1 mul.110
  110.3 0.1 mul.111
  110.4 0.6 gather_fusion
  111.0 0.1 bitcast_select_fusion.2
  111.1 7.3 %all-to-all-done.2 = bf16[1,2,1024,64]{2,1,0,3:T(2,128)(2,1)S(1)} async-done(((bf16[1,2,1024,64]{2,1,0,3:T(2,128)(2,1)}), bf16[1,2,1024,64]{2,1,0,3:T(2,128)(2,1)S(1)}, u32[]{:S(2)}, u32[]{:S(2)}) %all-to-all-start.2) | async-done | bytes 262176 | tf_op jit(solution)/shard_map/all_to_all | solution.py:147
  118.4 0.6 gather_fusion.2
  119.0 0.1 bitcast_select_fusion.1
  119.1 0.1 fusion.39
  119.1 0.6 multiply_add_fusion
  119.7 0.0 copy-start.1
  119.7 18.6 %fusion.1 = f32[1200,384]{1,0:T(8,128)S(1)} fusion(f32[1200,1024]{1,0:T(8,128)} %get-tuple-element.25, f32[1200,1024]{1,0:T(8,128)} %get-tuple-element.24, f32[1024,384]{0,1:T(8,128)S(1)} %bitcast.107, f32[1024,384]{0,1:T(8,128)S(1)} %bitcast.106, f32[384]{0:T(512)S(1)} %mul.111), kind=kOutput, calls=%fused_computation.7 | convolution fusion | flops 11331108864 | bytes 14820864 | tf_op jit(solution)/shard_map/dot_general | solution.py:94
  138.3 20.0 %fusion = f32[304,384]{1,0:T(8,128)S(1)} fusion(f32[1200,384]{1,0:T(8,128)S(1)} %fusion.1), kind=kCustom, calls=%all-reduce-scatter | all-reduce-scatter fusion | flops 466945 | bytes 2310656
  158.3 1.3 collective-permute-start
  159.6 0.6 dynamic-slice.10
  160.9 0.0 collective-permute-done
  160.9 0.5 concatenate.32
  161.4 0.8 constant_dynamic-slice_fusion
  (20 shorter events, 0.2 us)
Async XLA Ops:
  2.4 73.1 %all-to-all-start.1 = ((s32[4,1,2]{2,1,0:T(1,128)}), s32[4,1,2]{2,1,0:T(1,128)S(1)}, u32[]{:S(2)}, u32[]{:S(2)}) async-start(s32[4,1,2]{2,1,0:T(1,128)} %copy.28), calls=%async_computation.1 | async-start | bytes 4096 | tf_op jit(solution)/shard_map/all_to_all | solution.py:144
  15.4 38.0 %copy-start = (s32[2,6]{1,0:T(2,128)S(1)}, s32[2,6]{1,0:T(2,128)}, u32[]{:S(2)}) copy-start(s32[2,6]{1,0:T(2,128)} %param.6) | copy-start | bytes 148
  75.5 19.0 %all-to-all-start = ((bf16[4,2,32768]{2,1,0:T(2,128)(2,1)}), bf16[4,2,32768]{2,1,0:T(2,128)(2,1)S(1)}, u32[]{:S(2)}, u32[]{:S(2)}) async-start(bf16[4,2,32768]{2,1,0:T(2,128)(2,1)} %reshape.483), calls=%async_computation | async-start | bytes 1048576 | tf_op jit(solution)/shard_map/all_to_all | solution.py:107
  106.6 11.8 %all-to-all-start.2 = ((bf16[1,2,1024,64]{2,1,0,3:T(2,128)(2,1)}), bf16[1,2,1024,64]{2,1,0,3:T(2,128)(2,1)S(1)}, u32[]{:S(2)}, u32[]{:S(2)}) async-start(bf16[1,2,1024,64]{2,1,0,3:T(2,128)(2,1)} %copy.31), calls=%async_computation.2 | async-start | bytes 524288 | tf_op jit(solution)/shard_map/all_to_all | solution.py:147
  119.7 39.9 %copy-start.1 = (u32[32]{0:T(128)S(1)}, u32[32]{0:T(128)}, u32[]{:S(2)}) copy-start(u32[32]{0:T(128)} %constant.194) | copy-start | bytes 388
  158.3 2.5 %collective-permute-start = (f32[12,384]{1,0:T(8,128)S(1)}, f32[12,384]{1,0:T(8,128)S(1)}, u32[]{:S(2)}, u32[]{:S(2)}) collective-permute-start(f32[12,384]{1,0:T(8,128)S(1)} %slice.135), channel_id=1, source_target_pairs={{0,1},{1,2},{2,3},{4,5},{5,6},{6,7},{8,9},{9,10},{10,11},{12,13},{... | collective-permute-start | bytes 55304
where the time goes:
time: 165 us; the launch traced here: 162 us
  other arithmetic  67.9 us (41%)
  matrix products  26 us (16%)
  blocking collectives  20 us (12%)
  waiting for transfers between devices  18.4 us (11%)
  starting transfers between devices  16.3 us (10%)
  local copies, waits for them, and re-layouts  11.4 us (7%)
  between operations  2.26 us (1%)
    another operation x2, other arithmetic  36.9 us
    mul x1, other arithmetic, lag_offsets_table(): jnp.cos(angles) * weights  22 us
    unnamed x1, blocking collectives  20 us
    dot_general x1, matrix products, lag_sums(): jnp.dot(lag_rows, cross_terms, precision=lax.Precision.HIGHEST, preferred...  18.6 us
    all_to_all x1, waiting for transfers between devices, on_device(): lax.all_to_all(ingest, 'sta', split_axis=2, concat_axis=1, tiled=True)  11 us
    dot_general x1, matrix products, on_device(): jnp.einsum('kt,gts->gks', twiddles, whitened, preferred_element_type=jnp....  7.47 us
    all_to_all x1, waiting for transfers between devices, on_device(): lax.all_to_all(replies, 'sta', split_axis=3, concat_axis=3, tiled=True)  7.3 us
    unnamed x13, local copies, waits for them, and re-layouts  6.68 us
  transfers between devices with their start and end apart: 4, of which 2 were waited for; matrix products, arithmetic and copies ran while one was open for 43% of the time, Pallas kernels for 0%

commit v1 on v0

v1 whole, which is shorter than its diff:
```python
import functools
import math

import jax
import jax.numpy as jnp
import ml_dtypes
import numpy as np
from jax import lax
from jax.experimental import pallas as pl
from jax.experimental.pallas import tpu as pltpu
from jax.sharding import PartitionSpec as P

MAXLAG = 600
BLOCK = 8
HALF_TAPS = 10
FLOOR = 0.5
MESH = pl.DeviceIdType.MESH
F32 = jnp.float32
BF16 = jnp.bfloat16


def dft_tables(samples, bands):
    period = 2 * samples
    t = np.arange(samples)[:, None]
    tables = []
    for band in range(bands):
        k = np.arange(band, samples, bands)[None, :]
        angle = (k * t % period) * (2.0 * math.pi / period)
        tables.append(np.concatenate([np.cos(angle), -np.sin(angle)], 1))
    return np.stack(tables).astype(ml_dtypes.bfloat16)


def lag_tables(samples, bands, segments, groups, pad):
    period = 2 * samples
    per = 2 * MAXLAG // groups
    scale = 1.0 / (period * math.sqrt(samples * segments))
    tables = np.zeros((bands, groups, pad, 2 * samples // bands), np.float64)
    for band in range(bands):
        k = np.arange(band, samples, bands)[None, :]
        weight = np.where(k == 0, 1.0, 2.0) * scale
        tau = (np.arange(2 * MAXLAG) - MAXLAG)[:, None] % period
        angle = (k * tau % period) * (2.0 * math.pi / period)
        rows = np.concatenate([np.cos(angle) * weight, -np.sin(angle) * weight], 1)
        tables[band, :, :per] = rows.reshape(groups, per, -1)
    return tables.astype(ml_dtypes.bfloat16)


def kernel(
    owners, segs, slots, per,
    blocks_ref, count_ref, offset_ref, ingest_ref, dft_hbm, lag_hbm,
    out_ref,
    dft_v, lag_v, ids_v, traces_v, picked_v, white_v, cross_v,
    core_send, core_recv, seg_send, seg_recv,
    table_sem, ids_ssem, ids_rsem, tr_ssem, tr_rsem,
    wh_ssem, wh_rsem, core_ssem, core_rsem, seg_ssem, seg_rsem,
):
    z = lax.axis_index("sta")
    g = lax.axis_index("seg")
    f = lax.axis_index("frq")
    other = 1 - f
    rows, stations = ingest_ref.shape[1:]
    width = slots * BLOCK
    samples = rows * owners
    bins = samples // 2
    pad = lag_v.shape[1]

    dft_copy = pltpu.make_async_copy(dft_hbm.at[f], dft_v, table_sem.at[0])
    lag_copy = pltpu.make_async_copy(lag_hbm.at[f], lag_v, table_sem.at[1])
    dft_copy.start()
    lag_copy.start()

    sub = lax.broadcasted_iota(jnp.int32, (8, 128), 0)
    tile = jnp.zeros((8, 128), jnp.int32)
    for q in range(slots):
        tile = jnp.where(sub == q, blocks_ref[f, q], tile)
    ids_v[0] = tile

    barrier = pltpu.get_barrier_semaphore()
    for d in range(1, owners):
        pl.semaphore_signal(
            barrier, inc=1, device_id={"sta": lax.rem(z + d, owners)}, device_id_type=MESH
        )
    for d in range(1, segs):
        pl.semaphore_signal(
            barrier, inc=1, device_id={"seg": lax.rem(g + d, segs)}, device_id_type=MESH
        )
    pl.semaphore_signal(barrier, inc=1, device_id={"frq": other}, device_id_type=MESH)
    pl.semaphore_wait(barrier, owners + segs - 1)

    ids_copies = []
    for d in range(1, owners):
        copy = pltpu.make_async_remote_copy(
            src_ref=ids_v.at[0],
            dst_ref=ids_v.at[d],
            send_sem=ids_ssem.at[d],
            recv_sem=ids_rsem.at[d],
            device_id={"sta": lax.rem(z + d, owners)},
            device_id_type=MESH,
        )
        copy.start()
        ids_copies.append(copy)

    lane_station = lax.broadcasted_iota(jnp.int32, (8, stations), 1)
    sub_station = lax.broadcasted_iota(jnp.int32, (8, stations), 0)

    def pick(ids):
        hot = []
        for q in range(slots):
            block = jnp.broadcast_to(ids[q : q + 1, 0:1], (8, stations))
            hot.append((block * BLOCK + sub_station == lane_station).astype(F32))
        hot = jnp.concatenate(hot, 0).astype(BF16)
        picked = lax.dot_general(
            hot, ingest_ref[0], (((1,), (1,)), ((), ())), preferred_element_type=F32
        )
        return picked.astype(BF16)

    traces_v[z] = pick(tile)
    trace_copies = []
    for d in range(1, owners):
        ids_copies[d - 1].wait_recv()
        picked_v[d] = pick(ids_v[d])
        copy = pltpu.make_async_remote_copy(
            src_ref=picked_v.at[d],
            dst_ref=traces_v.at[z],
            send_sem=tr_ssem.at[d],
            recv_sem=tr_rsem.at[d],
            device_id={"sta": lax.rem(z + owners - d, owners)},
            device_id_type=MESH,
        )
        copy.start()
        trace_copies.append(copy)
    for copy in trace_copies:
        copy.wait_recv()

    offset = offset_ref[0]
    x = jnp.concatenate([traces_v[s] for s in range(owners)], 1).astype(F32)
    lane = lax.broadcasted_iota(jnp.int32, (width, samples), 1)
    t = lane - offset
    t = jnp.where(t < 0, t + samples, t)
    magnitude = jnp.abs(x)
    zero = jnp.zeros_like(magnitude)
    head = jnp.where(t < samples // 2, magnitude, zero)
    tail = jnp.where(t < samples // 2, zero, magnitude)
    halves = jnp.concatenate([head, tail], 0).astype(BF16)
    halves = jnp.concatenate([halves[:, samples - 128 :], halves, halves[:, :128]], 1)
    near = lax.broadcasted_iota(jnp.int32, (512, 256), 0) - 128
    near = near - lax.broadcasted_iota(jnp.int32, (512, 256), 1)
    band = (jnp.abs(near) <= HALF_TAPS).astype(F32).astype(BF16)
    for j in range(samples // 256):
        cols = slice(256 * j, 256 * j + 256)
        sums = jnp.dot(
            halves[:, 256 * j : 256 * j + 512], band, preferred_element_type=F32
        )
        head_sum, tail_sum = sums[:width], sums[width:]
        tj = t[:, cols]
        level = jnp.where(tj < samples // 4 * 3, head_sum, 0.0)
        level = level + jnp.where(tj >= samples // 4, tail_sum, 0.0)
        level = level / (2 * HALF_TAPS + 1)
        white_v[f, :, cols] = (x[:, cols] / jnp.maximum(level, FLOOR)).astype(BF16)

    white_copy = pltpu.make_async_remote_copy(
        src_ref=white_v.at[f],
        dst_ref=white_v.at[f],
        send_sem=wh_ssem,
        recv_sem=wh_rsem,
        device_id={"frq": other},
        device_id_type=MESH,
    )
    white_copy.start()
    dft_copy.wait()
    white_copy.wait_recv()

    flip = jnp.where((lane < offset) & (f == 1), -1.0, 1.0).astype(BF16)
    both = jnp.concatenate([white_v[0] * flip, white_v[1] * flip], 0)
    live = count_ref[0]
    for m in range(bins // 256):
        re = jnp.dot(both, dft_v[:, 256 * m : 256 * m + 256], preferred_element_type=F32)
        im = jnp.dot(
            both, dft_v[:, bins + 256 * m : bins + 256 * m + 256], preferred_element_type=F32
        )
        for q in range(slots):
            keep = jnp.where(q < live, 1.0, 0.0)
            first = slice(q * BLOCK, q * BLOCK + BLOCK)
            second = slice(width + q * BLOCK, width + q * BLOCK + BLOCK)
            a_re, a_im = re[first] * keep, im[first] * keep
            b_re, b_im = re[second], im[second]
            c_re, c_im = [], []
            for i in range(BLOCK):
                ar = jnp.broadcast_to(a_re[i : i + 1], (BLOCK, 256))
                ai = jnp.broadcast_to(a_im[i : i + 1], (BLOCK, 256))
                c_re.append(ar * b_re + ai * b_im)
                c_im.append(ai * b_re - ar * b_im)
            span = slice(q * BLOCK * BLOCK, (q + 1) * BLOCK * BLOCK)
            cross_v[span, 256 * m : 256 * m + 256] = jnp.concatenate(c_re, 0).astype(BF16)
            cross_v[span, bins + 256 * m : bins + 256 * m + 256] = jnp.concatenate(
                c_im, 0
            ).astype(BF16)

    lag_copy.wait()

    def lag_sums(seg, frq):
        return lax.dot_general(
            lag_v[seg * 2 + frq],
            cross_v[...],
            (((1,), (1,)), ((), ())),
            preferred_element_type=F32,
        )

    core_copies = []
    for j in range(segs):
        d = (j + 1) % segs
        seg = lax.rem(g + d, segs)
        core_send[d] = lag_sums(seg, other).astype(BF16)
        copy = pltpu.make_async_remote_copy(
            src_ref=core_send.at[d],
            dst_ref=core_recv.at[d],
            send_sem=core_ssem.at[d],
            recv_sem=core_rsem.at[d],
            device_id={"frq": other},
            device_id_type=MESH,
        )
        copy.start()
        core_copies.append(copy)
    seg_copies = []
    for d in range(1, segs):
        seg = lax.rem(g + d, segs)
        own = lag_sums(seg, f)
        core_copies[d - 1].wait_recv()
        seg_send[d] = (own + core_recv[d].astype(F32)).astype(BF16)
        copy = pltpu.make_async_remote_copy(
            src_ref=seg_send.at[d],
            dst_ref=seg_recv.at[d],
            send_sem=seg_ssem.at[d],
            recv_sem=seg_rsem.at[d],
            device_id={"seg": seg},
            device_id_type=MESH,
        )
        copy.start()
        seg_copies.append(copy)
    total = lag_sums(g, f)
    core_copies[segs - 1].wait_recv()
    total = total + core_recv[0].astype(F32)
    for d in range(1, segs):
        seg_copies[d - 1].wait_recv()
        total = total + seg_recv[d].astype(F32)
    out_ref[...] = total[:per]

    for copy in ids_copies + trace_copies + [white_copy] + core_copies + seg_copies:
        copy.wait_send()


def on_device(ingest, seg_offsets, pair_blocks, pair_count):
    owners = lax.axis_size("sta")
    segs = lax.axis_size("seg")
    bands = lax.axis_size("frq")
    groups = segs * bands
    _, rows, stations = ingest.shape
    samples = rows * owners
    slots = pair_blocks.shape[1]
    width = slots * BLOCK
    pairs = slots * BLOCK * BLOCK
    per = 2 * MAXLAG // groups
    pad = -(-per // 16) * 16
    dft = jnp.asarray(dft_tables(samples, bands))
    lags = jnp.asarray(lag_tables(samples, bands, segs, groups, pad))
    smem = pl.BlockSpec(memory_space=pltpu.SMEM)
    vmem = pl.BlockSpec(memory_space=pltpu.VMEM)
    hbm = pl.BlockSpec(memory_space=pl.ANY)
    dma = pltpu.SemaphoreType.DMA
    return pl.pallas_call(
        functools.partial(kernel, owners, segs, slots, per),
        out_shape=jax.ShapeDtypeStruct((per, pairs), F32),
        in_specs=[smem, smem, smem, vmem, hbm, hbm],
        out_specs=vmem,
        scratch_shapes=[
            pltpu.VMEM((samples, samples), BF16),
            pltpu.VMEM((groups, pad, samples), BF16),
            pltpu.VMEM((owners, 8, 128), jnp.int32),
            pltpu.VMEM((owners, width, rows), BF16),
            pltpu.VMEM((owners, width, rows), BF16),
            pltpu.VMEM((bands, width, samples), BF16),
            pltpu.VMEM((pairs, samples), BF16),
            pltpu.VMEM((segs, pad, pairs), BF16),
            pltpu.VMEM((segs, pad, pairs), BF16),
            pltpu.VMEM((segs, pad, pairs), BF16),
            pltpu.VMEM((segs, pad, pairs), BF16),
            dma((2,)),
            dma((owners,)),
            dma((owners,)),
            dma((owners,)),
            dma((owners,)),
            dma,
            dma,
            dma((segs,)),
            dma((segs,)),
            dma((segs,)),
            dma((segs,)),
        ],
        compiler_params=pltpu.CompilerParams(
            collective_id=0, has_side_effects=True, vmem_limit_bytes=48 * 1024 * 1024
        ),
    )(pair_blocks, pair_count, seg_offsets, ingest, dft, lags)


def solution(mesh):
    placed = (P(("win", "seg"), "sta", None), P(("win", "seg")), P(None, "sta"), P("sta"))
    return jax.shard_map(
        on_device,
        mesh=mesh,
        in_specs=placed,
        out_specs=P(("seg", "frq"), ("win", "sta")),
        check_vma=False,
    )
```

time: 165 us -> 31.7 us (0.19); the launches traced: 162 us -> 31.5 us
  other arithmetic: 67.9 us -> 0 us
  Pallas kernels: 0 us -> 27.7 us
  matrix products: 26 us -> 0 us
  blocking collectives: 20 us -> 0 us
  waiting for transfers between devices: 18.4 us -> 0 us
  starting transfers between devices: 16.3 us -> 0 us
  local copies, waits for them, and re-layouts: 11.4 us -> 2.49 us
    another operation x2 -> x0, other arithmetic: 36.9 us -> none
    pallas_call x0 -> x1, Pallas kernels: none -> 27.7 us  [on_device(): pl.pallas_call(functools.partial(kernel, owners, segs, slots, per), out_s...]
    dot_general x2 -> x0, matrix products: 26 us -> none  [the longest x1 18.6 us: lag_sums(): jnp.dot(lag_rows, cross_terms, precision=lax.Precision.HIGHEST, preferred...]
    mul x1 -> x0, other arithmetic: 22 us -> none  [lag_offsets_table(): jnp.cos(angles) * weights]
    unnamed x1 -> x0, blocking collectives: 20 us -> none
    all_to_all x3 -> x0, waiting for transfers between devices: 18.4 us -> none  [the longest x1 11 us: on_device(): lax.all_to_all(ingest, 'sta', split_axis=2, concat_axis=1, tiled=True)]
    all_to_all x3 -> x0, starting transfers between devices: 15 us -> none  [the longest x1 6.32 us: on_device(): lax.all_to_all(requests, 'sta', split_axis=0, concat_axis=0, tiled=True)]
    unnamed x13 -> x5, local copies, waits for them, and re-layouts: 6.68 us -> 2.49 us
  transfers between devices with their start and end apart: 4 -> 0, of which waited for: 2 -> 0; matrix products, arithmetic and copies ran while one was open for 43% -> 0% of each run, Pallas kernels for 0% -> 0%
where the time goes in v1:
time: 31.7 us; the launch traced here: 31.5 us
  Pallas kernels  27.7 us (87%)
  local copies, waits for them, and re-layouts  2.49 us (8%)
  between operations  1.31 us (4%)
    pallas_call x1, Pallas kernels, on_device(): pl.pallas_call(functools.partial(kernel, owners, segs, slots, per), out_s...  27.7 us
    unnamed x5, local copies, waits for them, and re-layouts  2.49 us

profile of v1, /device:TPU:0, one launch (start us, length us, event | category | flops | bytes accessed | tf_op | source)
XLA Modules:
  0.0 31.5 jit_solution(5264455834837778122)
XLA Ops:
  1.3 0.0 copy-start
  1.3 1.0 %copy-done = bf16[1,512,512]{2,1,0:T(8,128)(2,1)S(1)} copy-done((bf16[1,512,512]{2,1,0:T(8,128)(2,1)S(1)}, bf16[1,512,512]{2,1,0:T(8,128)(2,1)}, u32[]{:S(2)}) %copy-start) | copy-done | bytes 524312
  2.3 0.0 copy-start.1
  2.3 0.7 %copy-done.1 = s32[2,6]{1,0:T(2,128)S(1)} copy-done((s32[2,6]{1,0:T(2,128)S(1)}, s32[2,6]{1,0:T(2,128)}, u32[]{:S(2)}) %copy-start.1) | copy-done | bytes 72
  3.0 27.7 %shard_map.64 = f32[300,384]{1,0:T(8,128)S(1)} custom-call(s32[2,6]{1,0:T(2,128)S(1)} %copy-done.1, s32[1]{0:T(128)S(6)} %copy.9.count_ref, s32[1]{0:T(128)S(6)} %copy.8.offset_ref, bf16[1,512,512]{2,1,0:T(8,128)(2,1)S(1)} %copy-done, bf16[2,2048,2048]{2,1,0:T(8,128)(2,1)} %constant.4.clone.dft_hbm, bf16[2,4,304,2048]{3,2,1,0:T(8,128)(2,1)} %constant.5.clone.lag_hbm), custom_call_target="tpu_custom_call" | custom-call | tf_op jit(solution)/shard_map/pallas_call | solution.py:270
  30.7 0.8 %copy.10 = f32[300,384]{1,0:T(8,128)} copy(f32[300,384]{1,0:T(8,128)S(1)} %shard_map.64) | data formatting | bytes 921600
Async XLA Ops:
  1.3 1.0 %copy-start = (bf16[1,512,512]{2,1,0:T(8,128)(2,1)S(1)}, bf16[1,512,512]{2,1,0:T(8,128)(2,1)}, u32[]{:S(2)}) copy-start(bf16[1,512,512]{2,1,0:T(8,128)(2,1)} %ingest_ref.1) | copy-start | bytes 1572868
  2.3 0.7 %copy-start.1 = (s32[2,6]{1,0:T(2,128)S(1)}, s32[2,6]{1,0:T(2,128)}, u32[]{:S(2)}) copy-start(s32[2,6]{1,0:T(2,128)} %blocks_ref.1) | copy-start | bytes 148

commit v2 on v1

v2 whole, which is shorter than its diff:
```python
import functools
import math

import jax
import jax.numpy as jnp
import ml_dtypes
import numpy as np
from jax import lax
from jax.experimental import pallas as pl
from jax.experimental.pallas import tpu as pltpu
from jax.sharding import PartitionSpec as P

MAXLAG = 600
BLOCK = 8
HALF_TAPS = 10
FLOOR = 0.5
MESH = pl.DeviceIdType.MESH
F32 = jnp.float32
BF16 = jnp.bfloat16


def dft_tables(samples, bands):
    period = 2 * samples
    t = np.arange(samples)[:, None]
    tables = []
    for band in range(bands):
        k = np.arange(band, samples, bands)[None, :]
        angle = (k * t % period) * (2.0 * math.pi / period)
        tables.append(np.concatenate([np.cos(angle), -np.sin(angle)], 1))
    return np.stack(tables).astype(ml_dtypes.bfloat16)


def lag_tables(samples, bands, segments, segments_axis, pad):
    groups = segments_axis * bands
    period = 2 * samples
    per = 2 * MAXLAG // groups
    scale = 1.0 / (period * math.sqrt(samples * segments))
    tables = np.zeros((bands, groups, pad, 2 * samples // bands), np.float64)
    for band in range(bands):
        k = np.arange(band, samples, bands)[None, :]
        weight = np.where(k == 0, 1.0, 2.0) * scale
        tau = (np.arange(2 * MAXLAG) - MAXLAG)[:, None] % period
        angle = (k * tau % period) * (2.0 * math.pi / period)
        rows = np.concatenate([np.cos(angle) * weight, -np.sin(angle) * weight], 1)
        tables[band, :, :per] = rows.reshape(groups, per, -1)
    tables = tables.reshape(bands, segments_axis, bands, pad, -1)
    return tables.astype(ml_dtypes.bfloat16)


def kernel(
    owners, segs, slots, per,
    blocks_hbm, count_ref, offset_ref, ingest_hbm, dft_hbm, lag_hbm,
    out_ref,
    blocks_ref, ingest_ref, dft_v, lag_v, ids_v, off_v, traces_v, picked_v, white_v,
    cross_v, core_send, core_recv,
    table_sem, ids_ssem, ids_rsem, off_ssem, off_rsem, tr_ssem, tr_rsem,
    seg_ssem, seg_rsem, wh_ssem, wh_rsem, core_ssem, core_rsem,
):
    z = lax.axis_index("sta")
    g = lax.axis_index("seg")
    f = lax.axis_index("frq")
    other = 1 - f
    rows, stations = ingest_ref.shape[1:]
    width = slots * BLOCK
    samples = rows * owners
    bins = samples // 2

    blocks_copy = pltpu.make_async_copy(blocks_hbm, blocks_ref, table_sem.at[2])
    blocks_copy.start()
    ingest_copy = pltpu.make_async_copy(ingest_hbm, ingest_ref, table_sem.at[3])
    ingest_copy.start()
    dft_copy = pltpu.make_async_copy(dft_hbm.at[f], dft_v, table_sem.at[0])
    lag_copy = pltpu.make_async_copy(lag_hbm.at[f, g], lag_v, table_sem.at[1])
    dft_copy.start()
    lag_copy.start()

    barrier = pltpu.get_barrier_semaphore()
    for d in range(1, owners):
        pl.semaphore_signal(
            barrier, inc=1, device_id={"sta": lax.rem(z + d, owners)}, device_id_type=MESH
        )
    for d in range(1, segs):
        pl.semaphore_signal(
            barrier, inc=1, device_id={"seg": lax.rem(g + d, segs)}, device_id_type=MESH
        )
    pl.semaphore_signal(barrier, inc=1, device_id={"frq": other}, device_id_type=MESH)
    pl.semaphore_wait(barrier, owners + segs - 1)

    blocks_copy.wait()
    sub = lax.broadcasted_iota(jnp.int32, (8, 128), 0)
    tile = jnp.zeros((8, 128), jnp.int32)
    for q in range(slots):
        tile = jnp.where(sub == q, blocks_ref[f, q], tile)
    ids_v[0] = tile

    ids_copies = []
    for d in range(1, owners):
        copy = pltpu.make_async_remote_copy(
            src_ref=ids_v.at[0],
            dst_ref=ids_v.at[d],
            send_sem=ids_ssem.at[d],
            recv_sem=ids_rsem.at[d],
            device_id={"sta": lax.rem(z + d, owners)},
            device_id_type=MESH,
        )
        copy.start()
        ids_copies.append(copy)

    off_v[0] = jnp.full((8, 128), offset_ref[0], jnp.int32)
    off_copies = []
    for d in range(1, segs):
        copy = pltpu.make_async_remote_copy(
            src_ref=off_v.at[0],
            dst_ref=off_v.at[d],
            send_sem=off_ssem.at[d],
            recv_sem=off_rsem.at[d],
            device_id={"seg": lax.rem(g + d, segs)},
            device_id_type=MESH,
        )
        copy.start()
        off_copies.append(copy)

    lane_station = lax.broadcasted_iota(jnp.int32, (8, stations), 1)
    sub_station = lax.broadcasted_iota(jnp.int32, (8, stations), 0)

    def pick(ids):
        hot = []
        for q in range(slots):
            block = jnp.broadcast_to(ids[q : q + 1, 0:1], (8, stations))
            hot.append((block * BLOCK + sub_station == lane_station).astype(F32))
        hot = jnp.concatenate(hot, 0).astype(BF16)
        picked = lax.dot_general(
            hot, ingest_ref[0], (((1,), (1,)), ((), ())), preferred_element_type=F32
        )
        return picked.astype(BF16)

    seg_copies = [[] for _ in range(segs)]

    def pass_on(k):
        source = lax.rem(z + k, owners)
        for d in range(1, segs):
            copy = pltpu.make_async_remote_copy(
                src_ref=traces_v.at[0, source],
                dst_ref=traces_v.at[d, source],
                send_sem=seg_ssem.at[d, k],
                recv_sem=seg_rsem.at[d, k],
                device_id={"seg": lax.rem(g + d, segs)},
                device_id_type=MESH,
            )
            copy.start()
            seg_copies[d].append(copy)

    ingest_copy.wait()
    traces_v[0, z] = pick(tile)
    pass_on(0)
    trace_copies = []
    for d in range(1, owners):
        ids_copies[d - 1].wait_recv()
        picked_v[d] = pick(ids_v[d])
        copy = pltpu.make_async_remote_copy(
            src_ref=picked_v.at[d],
            dst_ref=traces_v.at[0, z],
            send_sem=tr_ssem.at[d],
            recv_sem=tr_rsem.at[d],
            device_id={"sta": lax.rem(z + owners - d, owners)},
            device_id_type=MESH,
        )
        copy.start()
        trace_copies.append(copy)
    for k in range(1, owners):
        trace_copies[k - 1].wait_recv()
        pass_on(k)

    near = lax.broadcasted_iota(jnp.int32, (512, 256), 0) - 128
    near = near - lax.broadcasted_iota(jnp.int32, (512, 256), 1)
    band = (jnp.abs(near) <= HALF_TAPS).astype(F32).astype(BF16)
    lane = lax.broadcasted_iota(jnp.int32, (1, samples), 1)

    def offset_row(d):
        return jnp.broadcast_to(off_v[d][0:1, 0:1], (1, samples))

    def whiten(d):
        x = jnp.concatenate([traces_v[d, s] for s in range(owners)], 1).astype(F32)
        t = lane - offset_row(d)
        t = jnp.where(t < 0, t + samples, t)
        magnitude = jnp.abs(x)
        is_head = (t < samples // 2).astype(F32)
        head = magnitude * is_head
        tail = magnitude - head
        halves = jnp.concatenate([head, tail], 0).astype(BF16)
        halves = jnp.concatenate([halves[:, samples - 128 :], halves, halves[:, :128]], 1)
        use_head = (t < samples // 4 * 3).astype(F32)
        use_tail = (t >= samples // 4).astype(F32)
        for j in range(samples // 256):
            cols = slice(256 * j, 256 * j + 256)
            sums = jnp.dot(
                halves[:, 256 * j : 256 * j + 512], band, preferred_element_type=F32
            )
            level = sums[:width] * use_head[:, cols] + sums[width:] * use_tail[:, cols]
            level = level / (2 * HALF_TAPS + 1)
            white_v[d, f, :, cols] = (x[:, cols] / jnp.maximum(level, FLOOR)).astype(BF16)

    white_copies = []
    for d in range(segs):
        if d:
            off_copies[d - 1].wait_recv()
            for copy in seg_copies[d]:
                copy.wait_recv()
        whiten(d)
        copy = pltpu.make_async_remote_copy(
            src_ref=white_v.at[d, f],
            dst_ref=white_v.at[d, f],
            send_sem=wh_ssem.at[d],
            recv_sem=wh_rsem.at[d],
            device_id={"frq": other},
            device_id_type=MESH,
        )
        copy.start()
        white_copies.append(copy)
    dft_copy.wait()

    both = []
    for d in range(segs):
        white_copies[d].wait_recv()
        flip = jnp.where((lane < offset_row(d)) & (f == 1), -1.0, 1.0)
        flip = jnp.broadcast_to(flip, (width, samples)).astype(BF16)
        both += [white_v[d, 0] * flip, white_v[d, 1] * flip]
    both = jnp.concatenate(both, 0)
    live = count_ref[0]
    for m in range(bins // 256):
        re = jnp.dot(both, dft_v[:, 256 * m : 256 * m + 256], preferred_element_type=F32)
        im = jnp.dot(
            both, dft_v[:, bins + 256 * m : bins + 256 * m + 256], preferred_element_type=F32
        )
        for q in range(slots):
            keep = jnp.where(q < live, 1.0, 0.0)
            c_re, c_im = [0.0] * BLOCK, [0.0] * BLOCK
            for d in range(segs):
                first = slice((2 * d * slots + q) * BLOCK, (2 * d * slots + q + 1) * BLOCK)
                second = slice(first.start + width, first.stop + width)
                a_re, a_im = re[first] * keep, im[first] * keep
                b_re, b_im = re[second], im[second]
                for i in range(BLOCK):
                    ar = jnp.broadcast_to(a_re[i : i + 1], (BLOCK, 256))
                    ai = jnp.broadcast_to(a_im[i : i + 1], (BLOCK, 256))
                    c_re[i] = c_re[i] + (ar * b_re + ai * b_im)
                    c_im[i] = c_im[i] + (ai * b_re - ar * b_im)
            span = slice(q * BLOCK * BLOCK, (q + 1) * BLOCK * BLOCK)
            cross_v[span, 256 * m : 256 * m + 256] = jnp.concatenate(c_re, 0).astype(BF16)
            cross_v[span, bins + 256 * m : bins + 256 * m + 256] = jnp.concatenate(
                c_im, 0
            ).astype(BF16)

    lag_copy.wait()

    def lag_sums(frq):
        return lax.dot_general(
            lag_v[frq], cross_v[...], (((1,), (1,)), ((), ())), preferred_element_type=F32
        )

    core_send[...] = lag_sums(other).astype(BF16)
    core_copy = pltpu.make_async_remote_copy(
        src_ref=core_send,
        dst_ref=core_recv,
        send_sem=core_ssem,
        recv_sem=core_rsem,
        device_id={"frq": other},
        device_id_type=MESH,
    )
    core_copy.start()
    total = lag_sums(f)
    core_copy.wait_recv()
    out_ref[...] = (total + core_recv[...].astype(F32))[:per]

    for copy in ids_copies + off_copies + trace_copies + sum(seg_copies, []):
        copy.wait_send()
    for copy in white_copies + [core_copy]:
        copy.wait_send()


def on_device(ingest, seg_offsets, pair_blocks, pair_count):
    owners = lax.axis_size("sta")
    segs = lax.axis_size("seg")
    bands = lax.axis_size("frq")
    groups = segs * bands
    _, rows, stations = ingest.shape
    samples = rows * owners
    slots = pair_blocks.shape[1]
    width = slots * BLOCK
    pairs = slots * BLOCK * BLOCK
    per = 2 * MAXLAG // groups
    pad = -(-per // 16) * 16
    dft = jnp.asarray(dft_tables(samples, bands))
    lags = jnp.asarray(lag_tables(samples, bands, segs, segs, pad))
    smem = pl.BlockSpec(memory_space=pltpu.SMEM)
    vmem = pl.BlockSpec(memory_space=pltpu.VMEM)
    hbm = pl.BlockSpec(memory_space=pl.ANY)
    dma = pltpu.SemaphoreType.DMA
    return pl.pallas_call(
        functools.partial(kernel, owners, segs, slots, per),
        out_shape=jax.ShapeDtypeStruct((per, pairs), F32),
        in_specs=[hbm, smem, smem, hbm, hbm, hbm],
        out_specs=vmem,
        scratch_shapes=[
            pltpu.SMEM(pair_blocks.shape, jnp.int32),
            pltpu.VMEM(ingest.shape, BF16),
            pltpu.VMEM((samples, samples), BF16),
            pltpu.VMEM((bands, pad, samples), BF16),
            pltpu.VMEM((owners, 8, 128), jnp.int32),
            pltpu.VMEM((segs, 8, 128), jnp.int32),
            pltpu.VMEM((segs, owners, width, rows), BF16),
            pltpu.VMEM((owners, width, rows), BF16),
            pltpu.VMEM((segs, bands, width, samples), BF16),
            pltpu.VMEM((pairs, samples), BF16),
            pltpu.VMEM((pad, pairs), BF16),
            pltpu.VMEM((pad, pairs), BF16),
            dma((4,)),
            dma((owners,)),
            dma((owners,)),
            dma((segs,)),
            dma((segs,)),
            dma((owners,)),
            dma((owners,)),
            dma((segs, owners)),
            dma((segs, owners)),
            dma((segs,)),
            dma((segs,)),
            dma,
            dma,
        ],
        compiler_params=pltpu.CompilerParams(
            collective_id=0, has_side_effects=True, vmem_limit_bytes=58 * 1024 * 1024
        ),
    )(pair_blocks, pair_count, seg_offsets, ingest, dft, lags)


def solution(mesh):
    placed = (P(("win", "seg"), "sta", None), P(("win", "seg")), P(None, "sta"), P("sta"))
    return jax.shard_map(
        on_device,
        mesh=mesh,
        in_specs=placed,
        out_specs=P(("seg", "frq"), ("win", "sta")),
        check_vma=False,
    )
```

time: 31.7 us -> 29.4 us (0.927)
  Pallas kernels: 27.7 us -> 26.1 us
  local copies, waits for them, and re-layouts: 2.49 us -> 1.82 us
    pallas_call x1, Pallas kernels: 27.7 us -> 26.1 us  [on_device(): pl.pallas_call(functools.partial(kernel, owners, segs, slots, per), out_s...]
    unnamed x5 -> x1, local copies, waits for them, and re-layouts: 2.49 us -> 1.82 us
where the time goes in v2:
time: 29.4 us; the launch traced here: 29.2 us
  Pallas kernels  26.1 us (89%)
  local copies, waits for them, and re-layouts  1.82 us (6%)
  between operations  1.3 us (4%)
    pallas_call x1, Pallas kernels, on_device(): pl.pallas_call(functools.partial(kernel, owners, segs, slots, per), out_s...  26.1 us
    unnamed x1, local copies, waits for them, and re-layouts  1.82 us

profile of v2, /device:TPU:0, one launch (start us, length us, event | category | flops | bytes accessed | tf_op | source)
XLA Modules:
  0.0 29.2 jit_solution(2464795752898537381)
XLA Ops:
  1.3 26.1 %shard_map.64 = f32[300,384]{1,0:T(8,128)} custom-call(s32[2,6]{1,0:T(2,128)} %blocks_hbm.1, s32[1]{0:T(128)S(6)} %copy.9.count_ref, s32[1]{0:T(128)S(6)} %copy.8.offset_ref, bf16[1,512,512]{2,1,0:T(8,128)(2,1)} %ingest_hbm.1, bf16[2,2048,2048]{2,1,0:T(8,128)(2,1)} %constant.4.clone.dft_hbm, bf16[2,2,2,304,2048]{4,3,2,1,0:T(8,128)(2,1)} %constant.5.clone.lag_hbm), custom_call_target="tpu_custom_call" | custom-call | tf_op jit(solution)/shard_map/pallas_call | solution.py:299
  27.4 1.8 %copy.10 = f32[300,384]{1,0:T(8,128)} copy(f32[300,384]{1,0:T(8,128)} %shard_map.64) | data formatting | bytes 921600

commit v3 on v2

--- a/solution.py
+++ b/solution.py
@@ -12,6 +12,7 @@
 
 MAXLAG = 600
 BLOCK = 8
+CHUNK = 16
 HALF_TAPS = 10
 FLOOR = 0.5
 MESH = pl.DeviceIdType.MESH
@@ -93,8 +94,11 @@
         tile = jnp.where(sub == q, blocks_ref[f, q], tile)
     ids_v[0] = tile
 
+    way = jnp.where(z < owners // 2, 1, owners - 1)
+    step = [lax.rem(way * j, owners) for j in range(owners)]
     ids_copies = []
-    for d in range(1, owners):
+    for j in range(owners - 1, 0, -1):
+        d = step[j]
         copy = pltpu.make_async_remote_copy(
             src_ref=ids_v.at[0],
             dst_ref=ids_v.at[d],
@@ -134,42 +138,53 @@
         )
         return picked.astype(BF16)
 
-    seg_copies = [[] for _ in range(segs)]
-
-    def pass_on(k):
+    parts = [pl.ds(CHUNK * c, CHUNK) for c in range(width // CHUNK)]
+    seg_copies = [[[] for _ in parts] for _ in range(segs)]
+
+    def pass_on(k, c):
         source = lax.rem(z + k, owners)
         for d in range(1, segs):
             copy = pltpu.make_async_remote_copy(
-                src_ref=traces_v.at[0, source],
-                dst_ref=traces_v.at[d, source],
-                send_sem=seg_ssem.at[d, k],
-                recv_sem=seg_rsem.at[d, k],
+                src_ref=traces_v.at[0, source, parts[c]],
+                dst_ref=traces_v.at[d, source, parts[c]],
+                send_sem=seg_ssem.at[d, k, c],
+                recv_sem=seg_rsem.at[d, k, c],
                 device_id={"seg": lax.rem(g + d, segs)},
                 device_id_type=MESH,
             )
             copy.start()
-            seg_copies[d].append(copy)
+            seg_copies[d][c].append(copy)
+
+    trace_copies = [[] for _ in parts]
+
+    def send_picked(d, c):
+        copy = pltpu.make_async_remote_copy(
+            src_ref=picked_v.at[d, parts[c]],
+            dst_ref=traces_v.at[0, z, parts[c]],
+            send_sem=tr_ssem.at[d, c],
+            recv_sem=tr_rsem.at[d, c],
+            device_id={"sta": lax.rem(z + owners - d, owners)},
+            device_id_type=MESH,
+        )
+        copy.start()
+        trace_copies[c].append(copy)
 
     ingest_copy.wait()
     traces_v[0, z] = pick(tile)
-    pass_on(0)
-    trace_copies = []
-    for d in range(1, owners):
-        ids_copies[d - 1].wait_recv()
+    for c in range(len(parts)):
+        pass_on(0, c)
+    for j in range(1, owners):
+        ids_copies[j - 1].wait_recv()
+        d = step[owners - j]
         picked_v[d] = pick(ids_v[d])
-        copy = pltpu.make_async_remote_copy(
-            src_ref=picked_v.at[d],
-            dst_ref=traces_v.at[0, z],
-            send_sem=tr_ssem.at[d],
-            recv_sem=tr_rsem.at[d],
-            device_id={"sta": lax.rem(z + owners - d, owners)},
-            device_id_type=MESH,
-        )
-        copy.start()
-        trace_copies.append(copy)
-    for k in range(1, owners):
-        trace_copies[k - 1].wait_recv()
-        pass_on(k)
+        send_picked(d, 0)
+    for c in range(1, len(parts)):
+        for j in range(1, owners):
+            send_picked(step[owners - j], c)
+    for c in range(len(parts)):
+        for j in range(1, owners):
+            trace_copies[c][owners - j - 1].wait_recv()
+            pass_on(step[j], c)
 
     near = lax.broadcasted_iota(jnp.int32, (512, 256), 0) - 128
     near = near - lax.broadcasted_iota(jnp.int32, (512, 256), 1)
@@ -179,8 +194,9 @@
     def offset_row(d):
         return jnp.broadcast_to(off_v[d][0:1, 0:1], (1, samples))
 
-    def whiten(d):
-        x = jnp.concatenate([traces_v[d, s] for s in range(owners)], 1).astype(F32)
+    def whiten(d, first, count):
+        span = slice(first, first + count)
+        x = jnp.concatenate([traces_v[d, s, span] for s in range(owners)], 1).astype(F32)
         t = lane - offset_row(d)
         t = jnp.where(t < 0, t + samples, t)
         magnitude = jnp.abs(x)
@@ -191,37 +207,47 @@
         halves = jnp.concatenate([halves[:, samples - 128 :], halves, halves[:, :128]], 1)
         use_head = (t < samples // 4 * 3).astype(F32)
         use_tail = (t >= samples // 4).astype(F32)
+        stacked = jnp.concatenate(
+            [halves[:, 256 * j : 256 * j + 512] for j in range(samples // 256)], 0
+        )
+        sums = jnp.dot(stacked, band, preferred_element_type=F32)
         for j in range(samples // 256):
             cols = slice(256 * j, 256 * j + 256)
-            sums = jnp.dot(
-                halves[:, 256 * j : 256 * j + 512], band, preferred_element_type=F32
-            )
-            level = sums[:width] * use_head[:, cols] + sums[width:] * use_tail[:, cols]
+            head_sum = sums[2 * j * count : (2 * j + 1) * count]
+            tail_sum = sums[(2 * j + 1) * count : (2 * j + 2) * count]
+            level = head_sum * use_head[:, cols] + tail_sum * use_tail[:, cols]
             level = level / (2 * HALF_TAPS + 1)
-            white_v[d, f, :, cols] = (x[:, cols] / jnp.maximum(level, FLOOR)).astype(BF16)
-
-    white_copies = []
-    for d in range(segs):
-        if d:
-            off_copies[d - 1].wait_recv()
-            for copy in seg_copies[d]:
+            white_v[d, f, span, cols] = (x[:, cols] / jnp.maximum(level, FLOOR)).astype(BF16)
+
+    white_copies = [[] for _ in range(segs)]
+
+    def swap_white(d, c, first, count):
+        copy = pltpu.make_async_remote_copy(
+            src_ref=white_v.at[d, f, pl.ds(first, count)],
+            dst_ref=white_v.at[d, f, pl.ds(first, count)],
+            send_sem=wh_ssem.at[d, c],
+            recv_sem=wh_rsem.at[d, c],
+            device_id={"frq": other},
+            device_id_type=MESH,
+        )
+        copy.start()
+        white_copies[d].append(copy)
+
+    whiten(0, 0, width)
+    swap_white(0, 0, 0, width)
+    for d in range(1, segs):
+        off_copies[d - 1].wait_recv()
+        for c in range(len(parts)):
+            for copy in seg_copies[d][c]:
                 copy.wait_recv()
-        whiten(d)
-        copy = pltpu.make_async_remote_copy(
-            src_ref=white_v.at[d, f],
-            dst_ref=white_v.at[d, f],
-            send_sem=wh_ssem.at[d],
-            recv_sem=wh_rsem.at[d],
-            device_id={"frq": other},
-            device_id_type=MESH,
-        )
-        copy.start()
-        white_copies.append(copy)
+            whiten(d, CHUNK * c, CHUNK)
+            swap_white(d, c, CHUNK * c, CHUNK)
     dft_copy.wait()
 
     both = []
     for d in range(segs):
-        white_copies[d].wait_recv()
+        for copy in white_copies[d]:
+            copy.wait_recv()
         flip = jnp.where((lane < offset_row(d)) & (f == 1), -1.0, 1.0)
         flip = jnp.broadcast_to(flip, (width, samples)).astype(BF16)
         both += [white_v[d, 0] * flip, white_v[d, 1] * flip]
@@ -253,28 +279,40 @@
 
     lag_copy.wait()
 
-    def lag_sums(frq):
+    def lag_sums(frq, first, count):
         return lax.dot_general(
-            lag_v[frq], cross_v[...], (((1,), (1,)), ((), ())), preferred_element_type=F32
-        )
-
-    core_send[...] = lag_sums(other).astype(BF16)
-    core_copy = pltpu.make_async_remote_copy(
-        src_ref=core_send,
-        dst_ref=core_recv,
-        send_sem=core_ssem,
-        recv_sem=core_rsem,
-        device_id={"frq": other},
-        device_id_type=MESH,
-    )
-    core_copy.start()
-    total = lag_sums(f)
-    core_copy.wait_recv()
-    out_ref[...] = (total + core_recv[...].astype(F32))[:per]
-
-    for copy in ids_copies + off_copies + trace_copies + sum(seg_copies, []):
-        copy.wait_send()
-    for copy in white_copies + [core_copy]:
+            lag_v[frq, first : first + count],
+            cross_v[...],
+            (((1,), (1,)), ((), ())),
+            preferred_element_type=F32,
+        )
+
+    pad = lag_v.shape[1]
+    cut = (pad // 2 + 15) // 16 * 16
+    core_copies = []
+    for h, (first, count) in enumerate([(0, cut), (cut, pad - cut)]):
+        core_send[first : first + count] = lag_sums(other, first, count).astype(BF16)
+        copy = pltpu.make_async_remote_copy(
+            src_ref=core_send.at[pl.ds(first, count)],
+            dst_ref=core_recv.at[pl.ds(first, count)],
+            send_sem=core_ssem.at[h],
+            recv_sem=core_rsem.at[h],
+            device_id={"frq": other},
+            device_id_type=MESH,
+        )
+        copy.start()
+        core_copies.append(copy)
+    total = lag_sums(f, 0, pad)
+    core_copies[0].wait_recv()
+    out_ref[:cut] = total[:cut] + core_recv[:cut].astype(F32)
+    core_copies[1].wait_recv()
+    out_ref[cut:] = (total[cut:] + core_recv[cut:].astype(F32))[: per - cut]
+
+    started = ids_copies + off_copies + core_copies
+    started += sum(trace_copies, []) + sum(white_copies, [])
+    for by_part in seg_copies:
+        started += sum(by_part, [])
+    for copy in started:
         copy.wait_send()
 
 
@@ -287,6 +325,7 @@
     samples = rows * owners
     slots = pair_blocks.shape[1]
     width = slots * BLOCK
+    chunks = width // CHUNK
     pairs = slots * BLOCK * BLOCK
     per = 2 * MAXLAG // groups
     pad = -(-per // 16) * 16
@@ -319,14 +358,14 @@
             dma((owners,)),
             dma((segs,)),
             dma((segs,)),
-            dma((owners,)),
-            dma((owners,)),
-            dma((segs, owners)),
-            dma((segs, owners)),
-            dma((segs,)),
-            dma((segs,)),
-            dma,
-            dma,
+            dma((owners, chunks)),
+            dma((owners, chunks)),
+            dma((segs, owners, chunks)),
+            dma((segs, owners, chunks)),
+            dma((segs, chunks)),
+            dma((segs, chunks)),
+            dma((2,)),
+            dma((2,)),
         ],
         compiler_params=pltpu.CompilerParams(
             collective_id=0, has_side_effects=True, vmem_limit_bytes=58 * 1024 * 1024

time: 29.4 us -> 28.9 us (0.983)
  Pallas kernels: 26.1 us -> 25.6 us
    pallas_call x1, Pallas kernels: 26.1 us -> 25.6 us  [on_device(): pl.pallas_call(functools.partial(kernel, owners, segs, slots, per), out_s...]
where the time goes in v3:
time: 28.9 us; the launch traced here: 28.7 us
  Pallas kernels  25.6 us (89%)
  local copies, waits for them, and re-layouts  1.82 us (6%)
  between operations  1.3 us (4%)
    pallas_call x1, Pallas kernels, on_device(): pl.pallas_call(functools.partial(kernel, owners, segs, slots, per), out_s...  25.6 us
    unnamed x1, local copies, waits for them, and re-layouts  1.82 us

profile of v3, /device:TPU:0, one launch (start us, length us, event | category | flops | bytes accessed | tf_op | source)
XLA Modules:
  0.0 28.7 jit_solution(4052478796489618455)
XLA Ops:
  1.3 25.6 %shard_map.64 = f32[300,384]{1,0:T(8,128)} custom-call(s32[2,6]{1,0:T(2,128)} %blocks_hbm.1, s32[1]{0:T(128)S(6)} %copy.9.count_ref, s32[1]{0:T(128)S(6)} %copy.8.offset_ref, bf16[1,512,512]{2,1,0:T(8,128)(2,1)} %ingest_hbm.1, bf16[2,2048,2048]{2,1,0:T(8,128)(2,1)} %constant.4.clone.dft_hbm, bf16[2,2,2,304,2048]{4,3,2,1,0:T(8,128)(2,1)} %constant.5.clone.lag_hbm), custom_call_target="tpu_custom_call" | custom-call | tf_op jit(solution)/shard_map/pallas_call | solution.py:338
  26.9 1.8 %copy.10 = f32[300,384]{1,0:T(8,128)} copy(f32[300,384]{1,0:T(8,128)} %shard_map.64) | data formatting | bytes 921600
